TPU v7x, 512 devices: a whole 4x8x8 slice. The times are simulated.
512 devices in a mesh: dp: 16 (over y, core), rule: 32 (over x, z).
Axes of the slice: x: 4, y: 8, z: 8, core: 2. Of those that a mesh axis runs over, the one named last changes fastest.
Arguments:
- hidden_states: bfloat16 [4096, 8192], P(('dp', 'rule')), may hold values from -6 to 6
- attn_input: bfloat16 [4096, 8192], P(('dp', 'rule')), may hold values from -6 to 6
- rule_ids: int32 [4096, 2], replicated, may hold values from 0 to 127, as said below
- slot_ids: int32 [4096, 2], replicated, may hold values from -1 to 127, as said below
- cotangent: bfloat16 [4096, 2], replicated, may hold values from -6 to 6
- adapter_in: bfloat16 [128, 8192, 512], P('dp', 'rule'), may hold values from -0.0625 to 0.0625
- adapter_bias: float32 [128, 512], P('dp'), may hold values from -3 to 3
- adapter_out: float32 [128, 512], P('dp'), may hold values from -0.25 to 0.25
Outputs:
- rewards: bfloat16 [4096, 2], P('dp')
- adapter_in_grad: bfloat16 [128, 8192, 512], P('dp', 'rule')
- adapter_bias_grad: float32 [128, 512], P('dp')
- adapter_out_grad: float32 [128, 512], P('dp')
- o_proj_grad: bfloat16 [8192, 8192], P('rule', 'dp')
Inputs may be any that keep to these rules, and one draw needn't show every extreme that they name: `rule_ids`: the owner of rule r is r // 8. Among the 16 pairs of one block of 8 consecutive tokens at most 2 name rules of any one owner, and in every block some owner gets exactly 2. The two rules of a token differ. slot_ids[t, k] counts the earlier pairs, in the order of t then k, that name the same rule; it is -1 where that count reaches 128. Some rule fills all 128 rows.
All inputs are finite; a program needn't handle non-finite values.
Results may differ from a plain program's by a relative error of at most 0.03.
Values may be sent and summed in bfloat16 or wider, within the bound.
No kernel may reach another device: no remote copies, remote signals or barrier semaphores. Data moves between devices by JAX's collectives and lax.ppermute only.
A program may use at most 64 MiB of HBM per device.

v0:
```python
import jax
import jax.numpy as jnp
from jax import lax
from jax.sharding import PartitionSpec as P


def local(
    hidden_states, attn_input, rule_ids, slot_ids, cotangent, adapter_in, adapter_bias, adapter_out
):
    dp_size = lax.axis_size("dp")
    rule_size = lax.axis_size("rule")
    dp_index = lax.axis_index("dp")
    rule_index = lax.axis_index("rule")
    rows_dev = hidden_states.shape[0]
    adapters, feature_cols, hidden_units = adapter_in.shape
    send_cap = max(2, 4 * rows_dev // dp_size)
    capacity = 4 * rows_dev * rule_size // adapters
    block_count = dp_size * rule_size
    pair_count = 2 * rows_dev
    slot_count = dp_size * send_cap
    recv_count = slot_count * rule_size
    buffer_rows = adapters * capacity
    rule_all = rule_ids.reshape(block_count, pair_count)
    slot_all = slot_ids.reshape(block_count, pair_count)
    cot_all = cotangent.reshape(block_count, pair_count).astype(jnp.float32)
    owner_all = rule_all // adapters
    earlier = jnp.arange(pair_count)[None, :] < jnp.arange(pair_count)[:, None]
    same_owner = owner_all[:, :, None] == owner_all[:, None, :]
    rank_all = jnp.sum((same_owner & earlier[None]).astype(jnp.int32), axis=2)
    my_block = dp_index * rule_size + rule_index
    my_owner = lax.dynamic_index_in_dim(owner_all, my_block, 0, keepdims=False)
    my_rank = lax.dynamic_index_in_dim(rank_all, my_block, 0, keepdims=False)
    target = my_owner * send_cap + my_rank
    select_pairs = (jnp.arange(slot_count)[:, None] == target[None, :]).astype(jnp.int32)
    select_tokens = jnp.sum(select_pairs.reshape(slot_count, rows_dev, 2), axis=2).astype(
        jnp.bfloat16
    )
    outgoing = jnp.dot(select_tokens, hidden_states, preferred_element_type=jnp.float32).astype(
        jnp.bfloat16
    )
    outgoing = outgoing.reshape(dp_size, send_cap, rule_size, feature_cols)
    incoming = lax.all_to_all(
        lax.all_to_all(outgoing, "dp", split_axis=0, concat_axis=0, tiled=True),
        "rule",
        split_axis=2,
        concat_axis=2,
        tiled=True,
    )
    flat_in = jnp.concatenate(
        [incoming.reshape(recv_count, feature_cols), jnp.zeros((1, feature_cols), jnp.bfloat16)],
        axis=0,
    )
    block_dp = (jnp.arange(block_count) // rule_size)[:, None]
    block_rule = (jnp.arange(block_count) % rule_size)[:, None]
    recv_index = (block_dp * send_cap + rank_all) * rule_size + block_rule
    owned = (owner_all == dp_index) & (slot_all >= 0)
    buffer_pos = rule_all % adapters * capacity + slot_all
    pos_target = jnp.where(owned, buffer_pos, buffer_rows).reshape(-1)
    recv_target = jnp.where(owned, recv_index, recv_count).reshape(-1)
    to_recv = (
        jnp.full((buffer_rows + 1,), recv_count, jnp.int32)
        .at[pos_target]
        .set(recv_index.reshape(-1))[:buffer_rows]
    )
    to_buffer = (
        jnp.full((recv_count + 1,), buffer_rows, jnp.int32)
        .at[recv_target]
        .set(buffer_pos.reshape(-1))[:recv_count]
    )
    cot_buffer = (
        jnp.zeros((buffer_rows + 1,), jnp.float32)
        .at[pos_target]
        .set(cot_all.reshape(-1))[:buffer_rows]
    )
    cot_rows = cot_buffer.reshape(adapters, capacity)
    rows_buf = jnp.take(flat_in, to_recv, axis=0).reshape(adapters, capacity, feature_cols)
    partial_pre = jnp.einsum(
        "acd,adr->acr", rows_buf, adapter_in, preferred_element_type=jnp.float32
    )
    preact = (
        lax.psum(partial_pre.astype(jnp.bfloat16), "rule").astype(jnp.float32)
        + adapter_bias[:, None, :]
    )
    sigmoid_z = jax.nn.sigmoid(preact)
    activated = preact * sigmoid_z
    reward_rows = jnp.sum(activated * adapter_out[:, None, :], axis=2)
    grad_pre = (
        cot_rows[:, :, None]
        * adapter_out[:, None, :]
        * sigmoid_z
        * (1.0 + preact * (1.0 - sigmoid_z))
    )
    grad_half = grad_pre.astype(jnp.bfloat16)
    bias_grad = jnp.sum(grad_pre, axis=1)
    out_grad = jnp.sum(cot_rows[:, :, None] * activated, axis=1)
    reward_flat = jnp.concatenate([reward_rows.reshape(-1), jnp.zeros((1,), jnp.float32)]).astype(
        jnp.bfloat16
    )
    in_grad = jnp.einsum(
        "acd,acr->adr", rows_buf, grad_half, preferred_element_type=jnp.float32
    ).astype(jnp.bfloat16)
    input_grad = jnp.einsum(
        "acr,adr->acd", grad_half, adapter_in, preferred_element_type=jnp.float32
    ).astype(jnp.bfloat16)
    grad_flat = jnp.concatenate(
        [input_grad.reshape(buffer_rows, feature_cols), jnp.zeros((1, feature_cols), jnp.bfloat16)],
        axis=0,
    )
    back_rows = jnp.take(grad_flat, to_buffer, axis=0).reshape(
        dp_size, send_cap, rule_size, feature_cols
    )
    back_reward = jnp.take(reward_flat, to_buffer, axis=0).reshape(dp_size, send_cap, rule_size)
    returned, reward_back = (
        lax.all_to_all(back_rows, "dp", split_axis=0, concat_axis=0, tiled=True),
        lax.all_to_all(back_reward, "dp", split_axis=0, concat_axis=0, tiled=True),
    )
    owner_group = lax.dynamic_slice_in_dim(owner_all, dp_index * rule_size, rule_size, 0)
    rank_group = lax.dynamic_slice_in_dim(rank_all, dp_index * rule_size, rule_size, 0)
    pair_index = (
        (owner_group * send_cap + rank_group) * rule_size + jnp.arange(rule_size)[:, None]
    ).reshape(-1)
    pair_grads = jnp.take(returned.reshape(recv_count, feature_cols), pair_index, axis=0)
    pair_grads = pair_grads.astype(jnp.float32).reshape(rule_size * rows_dev, 2, feature_cols)
    state_grad = jnp.sum(pair_grads, axis=1).astype(jnp.bfloat16)
    rewards = jnp.take(reward_back.reshape(recv_count), pair_index, axis=0).reshape(
        rule_size * rows_dev, 2
    )
    group_term = lax.dot_general(
        state_grad,
        lax.all_gather(attn_input, "rule", axis=0, tiled=True),
        (((0,), (0,)), ((), ())),
        preferred_element_type=jnp.float32,
    )
    o_proj_grad = lax.psum_scatter(
        group_term.astype(jnp.bfloat16), "dp", scatter_dimension=1, tiled=True
    )
    return (rewards, in_grad, bias_grad, out_grad, o_proj_grad)


def solution(mesh):
    placed = (
        P(("dp", "rule"), None),
        P(("dp", "rule"), None),
        P(),
        P(),
        P(),
        P("dp", "rule", None),
        P("dp", None),
        P("dp", None),
    )
    return jax.shard_map(
        local,
        mesh=mesh,
        in_specs=placed,
        out_specs=(
            P("dp", None),
            P("dp", "rule", None),
            P("dp", None),
            P("dp", None),
            P("rule", "dp"),
        ),
        check_vma=False,
    )
```

profile of v0, /device:TPU:25, one launch (start us, length us, event | category | flops | bytes accessed | tf_op | source)
XLA Modules:
  0.0 413.3 jit_solution(5841563843183169320)
XLA Ops:
  7.2 2.9 copy.44
  10.1 2.2 reshape.437
  14.8 9.4 %all-to-all-start = ((bf16[16,2,32,256]{3,1,2,0:T(2,128)(2,1)}), bf16[16,2,32,256]{3,1,2,0:T(2,128)(2,1)S(1)}, u32[]{:S(2)}, u32[]{:S(2)}) async-start(bf16[16,2,32,256]{3,1,2,0:T(2,128)(2,1)} %copy.57), calls=%async_computation | async-start | bytes 1048576 | tf_op jit(solution)/shard_map/all_to_all | solution.py:43
  24.3 3.0 reshape.439
  27.6 2.0 copy.51
  29.6 3.0 reshape.440
  32.9 6.3 %all-to-all-done = bf16[16,2,32,256]{3,1,2,0:T(2,128)(2,1)S(1)} async-done(((bf16[16,2,32,256]{3,1,2,0:T(2,128)(2,1)}), bf16[16,2,32,256]{3,1,2,0:T(2,128)(2,1)S(1)}, u32[]{:S(2)}, u32[]{:S(2)}) %all-to-all-start) | async-done | bytes 524320 | tf_op jit(solution)/shard_map/all_to_all | solution.py:43
  40.6 11.2 %all-to-all-start.1 = ((bf16[16,2,32,256]{3,1,0,2:T(2,128)(2,1)}), bf16[16,2,32,256]{3,1,0,2:T(2,128)(2,1)S(1)}, u32[]{:S(2)}, u32[]{:S(2)}) async-start(bf16[16,2,32,256]{3,1,0,2:T(2,128)(2,1)} %copy.58), calls=%async_computation.1 | async-start | bytes 1048576 | tf_op jit(solution)/shard_map/all_to_all | solution.py:42
  52.2 30.4 %scatter_custom_fusion.1 = s32[1025]{0:T(1024)S(1)} fusion(s32[8192]{0:T(1024)S(1)} %bitcast.35, s32[8192]{0:T(1024)S(1)} %reshape.505, s32[]{:T(128)} %constant.137.clone.1), kind=kCustom, calls=%fused_computation.76 | custom fusion | bytes 4104 | tf_op jit(solution)/shard_map/scatter | solution.py:63
  83.0 4.9 %gather_fusion.3 = bf16[1024,256]{1,0:T(8,128)(2,1)} fusion(bf16[1025,256]{1,0:T(8,128)(2,1)S(1)} %concatenate.10, s32[1024]{0:T(1024)S(1)} %fusion.23), kind=kCustom, calls=%fused_computation.clone | custom fusion | bytes 1052672 | tf_op jit(solution)/shard_map/jit(_take)/gather | solution.py:76
  91.5 2.7 reshape.441
  94.2 2.7 reshape.442
  97.0 30.4 %scatter_custom_fusion = s32[1025]{0:T(1024)S(1)} fusion(s32[8192]{0:T(1024)S(1)} %bitcast.34, s32[8192]{0:T(1024)S(1)} %fusion.7, s32[]{:T(128)} %constant.137.clone.1), kind=kCustom, calls=%fused_computation.78 | custom fusion | bytes 4104 | tf_op jit(solution)/shard_map/scatter | solution.py:68
  127.6 1.7 copy.61
  129.3 2.7 reshape.513
  132.0 30.4 %scatter_custom_fusion.2 = f32[1025]{0:T(1024)S(1)} fusion(s32[8192]{0:T(1024)S(1)} %bitcast.36, f32[8192]{0:T(1024)S(1)} %reshape.513, f32[]{:T(128)} %constant.147.clone.1), kind=kCustom, calls=%fused_computation.67 | custom fusion | bytes 4104 | tf_op jit(solution)/shard_map/scatter | solution.py:73
  162.5 83.6 %all-reduce.4.cloned.1.call-done = bf16[8,128,512]{2,1,0:T(8,128)(2,1)} async-done(((bf16[8,128,512]{2,1,0:T(8,128)(2,1)}), bf16[8,128,512]{2,1,0:T(8,128)(2,1)}) %all-reduce.4.cloned.1.call-update) | async-done | bytes 1048592 | tf_op jit(solution)/shard_map/psum | solution.py:81
  246.1 3.4 fusion.29
  249.5 6.8 %gather_fusion = bf16[1024]{0:T(1024)(128)(2,1)S(1)} fusion(bf16[1025]{0:T(1024)(128)(2,1)S(1)} %pad_maximum_fusion, s32[1024]{0:T(1024)S(1)} %get-tuple-element.34), kind=kCustom, calls=%fused_computation.2 | custom fusion | bytes 8192 | tf_op jit(solution)/shard_map/jit(_take)/gather | solution.py:112
  257.0 12.1 %all-to-all-start.2 = ((bf16[16,2,32]{2,1,0:T(2,128)(2,1)}), bf16[16,2,32]{2,1,0:T(2,128)(2,1)S(1)}, u32[]{:S(2)}, u32[]{:S(2)}) async-start(bf16[16,2,32]{2,1,0:T(2,128)(2,1)} %and_select_fusion.2), calls=%async_computation.2 | async-start | bytes 16384 | tf_op jit(solution)/shard_map/all_to_all | solution.py:115
  269.1 2.3 convolution_convert_fusion.4
  271.5 5.0 %gather_fusion.4 = bf16[1024,256]{1,0:T(8,128)(2,1)} fusion(bf16[1025,256]{1,0:T(8,128)(2,1)S(1)} %concatenate.12, s32[1024]{0:T(1024)S(1)} %get-tuple-element.34), kind=kCustom, calls=%fused_computation.1.clone | custom fusion | bytes 1052672 | tf_op jit(solution)/shard_map/jit(_take)/gather | solution.py:109
  276.5 2.0 broadcast_select_fusion
  278.6 7.2 %all-to-all-start.3 = ((bf16[16,2,32,256]{3,2,1,0:T(8,128)(2,1)}), bf16[16,2,32,256]{3,2,1,0:T(8,128)(2,1)S(1)}, u32[]{:S(2)}, u32[]{:S(2)}) async-start(bf16[16,2,32,256]{3,2,1,0:T(8,128)(2,1)} %bitcast.29), calls=%async_computation.3 | async-start | bytes 1048576 | tf_op jit(solution)/shard_map/all_to_all | solution.py:114
  286.5 3.5 gather_fusion.1
  290.3 10.5 %all-to-all-done.3 = bf16[16,2,32,256]{3,2,1,0:T(8,128)(2,1)S(1)} async-done(((bf16[16,2,32,256]{3,2,1,0:T(8,128)(2,1)}), bf16[16,2,32,256]{3,2,1,0:T(8,128)(2,1)S(1)}, u32[]{:S(2)}, u32[]{:S(2)}) %all-to-all-start.3) | async-done | bytes 524320 | tf_op jit(solution)/shard_map/all_to_all | solution.py:114
  300.8 1.9 gather_fusion.2
  302.8 2.0 fusion.3
  304.8 31.3 %all-gather.2.cloned.1.call-done = bf16[256,8192]{1,0:T(8,128)(2,1)} async-done(((bf16[8,8192]{1,0:T(8,128)(2,1)}), bf16[256,8192]{1,0:T(8,128)(2,1)}) %all-gather.2.cloned.1.call-update) | async-done | bytes 4194320 | tf_op jit(solution)/shard_map/all_gather | solution.py:130
  336.2 5.4 %convolution_convert_fusion = bf16[256,8192]{1,0:T(8,128)(2,1)} fusion(bf16[256,256]{1,0:T(8,128)(2,1)S(1)} %fusion.3, bf16[256,8192]{1,0:T(8,128)(2,1)} %all-gather.2.cloned.1.call-done), kind=kOutput, calls=%fused_computation.8 | convolution fusion | flops 1075838976 | bytes 8519680 | tf_op jit(solution)/shard_map/dot_general | solution.py:128
  341.6 3.8 convolution_convert_fusion.2
  346.1 60.7 %reduce-scatter.2.cloned.1.call-done = bf16[256,512]{1,0:T(8,128)(2,1)} async-done(((bf16[256,8192]{1,0:T(8,128)(2,1)}), bf16[256,512]{1,0:T(8,128)(2,1)}) %reduce-scatter.2.cloned.1.call-update) | async-done | bytes 262160 | tf_op jit(solution)/shard_map/reduce_scatter | solution.py:134
  (65 shorter events, 11.1 us)
Async XLA Ops:
  7.2 82.1 %copy-start = (bf16[8,256,512]{2,1,0:T(8,128)(2,1)S(1)}, bf16[8,256,512]{2,1,0:T(8,128)(2,1)}, u32[]{:S(2)}) copy-start(bf16[8,256,512]{2,1,0:T(8,128)(2,1)} %param.15) | copy-start | bytes 6291460
  7.2 5.8 %copy-start.1 = (bf16[8,8192]{1,0:T(8,128)(2,1)S(1)}, bf16[8,8192]{1,0:T(8,128)(2,1)}, u32[]{:S(2)}) copy-start(bf16[8,8192]{1,0:T(8,128)(2,1)} %param.10) | copy-start | bytes 393220
  14.8 12.8 %copy-start.2 = (s32[4096,2]{0,1:T(2,128)S(1)}, s32[4096,2]{0,1:T(2,128)}, u32[]{:S(2)}) copy-start(s32[4096,2]{0,1:T(2,128)} %param.13) | copy-start | bytes 98308
  14.8 24.4 %all-to-all-start = ((bf16[16,2,32,256]{3,1,2,0:T(2,128)(2,1)}), bf16[16,2,32,256]{3,1,2,0:T(2,128)(2,1)S(1)}, u32[]{:S(2)}, u32[]{:S(2)}) async-start(bf16[16,2,32,256]{3,1,2,0:T(2,128)(2,1)} %copy.57), calls=%async_computation | async-start | bytes 1048576 | tf_op jit(solution)/shard_map/all_to_all | solution.py:43
  40.6 42.1 %all-to-all-start.1 = ((bf16[16,2,32,256]{3,1,0,2:T(2,128)(2,1)}), bf16[16,2,32,256]{3,1,0,2:T(2,128)(2,1)S(1)}, u32[]{:S(2)}, u32[]{:S(2)}) async-start(bf16[16,2,32,256]{3,1,0,2:T(2,128)(2,1)} %copy.58), calls=%async_computation.1 | async-start | bytes 1048576 | tf_op jit(solution)/shard_map/all_to_all | solution.py:42
  51.8 194.3 %all-reduce.4.cloned.1.call-start = ((), (), s32[]{:S(2)}) async-start(), calls=%async_computation.5 | async-start | bytes 2097152 | tf_op jit(solution)/shard_map/psum | solution.py:81
  90.7 245.4 %all-gather.2.cloned.1.call-start = ((), (), s32[]{:S(2)}) async-start(), calls=%async_computation.6 | async-start | bytes 4325376 | tf_op jit(solution)/shard_map/all_gather | solution.py:130
  91.5 36.1 %copy-start.3 = (bf16[4096,2]{0,1:T(2,128)(2,1)S(1)}, bf16[4096,2]{0,1:T(2,128)(2,1)}, u32[]{:S(2)}) copy-start(bf16[4096,2]{0,1:T(2,128)(2,1)} %param.14) | copy-start | bytes 49156
  127.5 118.6 %copy-start.4 = (f32[8,512]{1,0:T(8,128)S(1)}, f32[8,512]{1,0:T(8,128)}, u32[]{:S(2)}) copy-start(f32[8,512]{1,0:T(8,128)} %param.16) | copy-start | bytes 49156
  127.5 118.6 %copy-start.5 = (f32[8,512]{1,0:T(8,128)S(1)}, f32[8,512]{1,0:T(8,128)}, u32[]{:S(2)}) copy-start(f32[8,512]{1,0:T(8,128)} %param.17) | copy-start | bytes 49156
  257.0 21.5 %all-to-all-start.2 = ((bf16[16,2,32]{2,1,0:T(2,128)(2,1)}), bf16[16,2,32]{2,1,0:T(2,128)(2,1)S(1)}, u32[]{:S(2)}, u32[]{:S(2)}) async-start(bf16[16,2,32]{2,1,0:T(2,128)(2,1)} %and_select_fusion.2), calls=%async_computation.2 | async-start | bytes 16384 | tf_op jit(solution)/shard_map/all_to_all | solution.py:115
  278.6 22.2 %all-to-all-start.3 = ((bf16[16,2,32,256]{3,2,1,0:T(8,128)(2,1)}), bf16[16,2,32,256]{3,2,1,0:T(8,128)(2,1)S(1)}, u32[]{:S(2)}, u32[]{:S(2)}) async-start(bf16[16,2,32,256]{3,2,1,0:T(8,128)(2,1)} %bitcast.29), calls=%async_computation.3 | async-start | bytes 1048576 | tf_op jit(solution)/shard_map/all_to_all | solution.py:114
  285.8 121.0 %reduce-scatter.2.cloned.1.call-start = ((), (), s32[]{:S(2)}) async-start(), calls=%async_computation.7 | async-start | bytes 4456448 | tf_op jit(solution)/shard_map/reduce_scatter | solution.py:134
Sparse Core Ops, SparseCore 0:
  90.8 155.2 all-reduce.3
  249.3 86.8 all-gather.1
  341.7 65.0 reduce-scatter.1
where the time goes:
time: 414 us; the launch traced here: 413 us
  waiting for transfers between devices  193 us (47%)
  local copies, waits for them, and re-layouts  142 us (34%)
  starting transfers between devices  40.5 us (10%)
  between operations  14.1 us (3%)
  matrix products  13.4 us (3%)
  other arithmetic  10.4 us (3%)
    psum x1, waiting for transfers between devices, local(): lax.psum(partial_pre.astype(jnp.bfloat16), 'rule').astype(jnp.float32)  83.6 us
    reduce_scatter x1, waiting for transfers between devices, local(): lax.psum_scatter(group_term.astype(jnp.bfloat16), 'dp', scatter_dimension...  60.7 us
    all_gather x1, waiting for transfers between devices, local(): lax.all_gather(attn_input, 'rule', axis=0, tiled=True)  31.3 us
    scatter x1, local copies, waits for them, and re-layouts, local(): to_recv = jnp.full((buffer_rows + 1,), recv_count, jnp.int32).at[pos_targ...  30.4 us
    scatter x1, local copies, waits for them, and re-layouts, local(): to_buffer = jnp.full((recv_count + 1,), buffer_rows, jnp.int32).at[recv_t...  30.4 us
    scatter x1, local copies, waits for them, and re-layouts, local(): cot_buffer = jnp.zeros((buffer_rows + 1,), jnp.float32).at[pos_target].se...  30.4 us
    all_to_all x1, starting transfers between devices, local(): lax.all_to_all(back_reward, 'dp', split_axis=0, concat_axis=0, tiled=True)  12.1 us
    all_to_all x1, starting transfers between devices, local(): lax.all_to_all(lax.all_to_all(outgoing, 'dp', split_axis=0, concat_axis=0...  11.2 us
  transfers between devices with their start and end apart: 7, of which 5 were waited for; matrix products, arithmetic and copies ran while one was open for 35% of the time, Pallas kernels for 0%

commit v1 on v0

--- a/solution.py
+++ b/solution.py
@@ -2,6 +2,29 @@
 import jax.numpy as jnp
 from jax import lax
 from jax.sharding import PartitionSpec as P
+
+
+def in_blocks(x, dim, size):
+    before, after = (x.shape[:dim], x.shape[dim + 1 :])
+    return jnp.moveaxis(x.reshape(*before, size, -1, *after), dim, 0)
+
+
+def joined_along(blocks, dim):
+    shape = list(blocks.shape[1:])
+    shape[dim] *= blocks.shape[0]
+    return jnp.moveaxis(blocks, 0, dim).reshape(shape)
+
+
+def exchange_directly(x, axis, split_dim, concat_dim):
+    size, index = (lax.axis_size(axis), lax.axis_index(axis))
+    blocks = in_blocks(x, split_dim, size)
+    out = blocks
+    for step in range(1, size):
+        target, source = ((index + step) % size, (index - step) % size)
+        sent = lax.dynamic_index_in_dim(blocks, target, 0)
+        partner_block = lax.ppermute(sent, axis, [(i, (i + step) % size) for i in range(size)])
+        out = lax.dynamic_update_slice_in_dim(out, partner_block, source, axis=0)
+    return joined_along(out, concat_dim)
 
 
 def local(
@@ -40,11 +63,7 @@
     )
     outgoing = outgoing.reshape(dp_size, send_cap, rule_size, feature_cols)
     incoming = lax.all_to_all(
-        lax.all_to_all(outgoing, "dp", split_axis=0, concat_axis=0, tiled=True),
-        "rule",
-        split_axis=2,
-        concat_axis=2,
-        tiled=True,
+        exchange_directly(outgoing, "dp", 0, 0), "rule", split_axis=2, concat_axis=2, tiled=True
     )
     flat_in = jnp.concatenate(
         [incoming.reshape(recv_count, feature_cols), jnp.zeros((1, feature_cols), jnp.bfloat16)],

time: 414 us -> 466 us (1.13)
  the two profiles are of different devices: /device:TPU:25 before, /device:TPU:6 now
where the time goes in v1:
time: 466 us; the launch traced here: 465 us
  waiting for transfers between devices  189 us (41%)
  local copies, waits for them, and re-layouts  156 us (33%)
  starting transfers between devices  81.5 us (17%)
  between operations  14.9 us (3%)
  matrix products  13.4 us (3%)
  other arithmetic  10.4 us (2%)
    psum x1, waiting for transfers between devices, local(): lax.psum(partial_pre.astype(jnp.bfloat16), 'rule').astype(jnp.float32)  84.3 us
    reduce_scatter x1, waiting for transfers between devices, local(): lax.psum_scatter(group_term.astype(jnp.bfloat16), 'dp', scatter_dimension...  58.9 us
    ppermute x15, starting transfers between devices, exchange_directly(): lax.ppermute(sent, axis, [(i, (i + step) % size) for i in range(size)])  53.5 us
    all_gather x1, waiting for transfers between devices, local(): lax.all_gather(attn_input, 'rule', axis=0, tiled=True)  34 us
    scatter x1, local copies, waits for them, and re-layouts, local(): to_recv = jnp.full((buffer_rows + 1,), recv_count, jnp.int32).at[pos_targ...  30.4 us
    scatter x1, local copies, waits for them, and re-layouts, local(): to_buffer = jnp.full((recv_count + 1,), buffer_rows, jnp.int32).at[recv_t...  30.4 us
    scatter x1, local copies, waits for them, and re-layouts, local(): cot_buffer = jnp.zeros((buffer_rows + 1,), jnp.float32).at[pos_target].se...  30.4 us
    all_to_all x1, starting transfers between devices, local(): lax.all_to_all(exchange_directly(outgoing, 'dp', 0, 0), 'rule', split_axi...  13.5 us
  transfers between devices with their start and end apart: 21, of which 4 were waited for; matrix products, arithmetic and copies ran while one was open for 34% of the time, Pallas kernels for 0%

profile of v1, /device:TPU:6, one launch (start us, length us, event | category | flops | bytes accessed | tf_op | source)
XLA Modules:
  0.0 465.1 jit_solution(11249828814003891096)
XLA Ops:
  7.4 2.9 copy.48
  15.1 3.5 collective-permute-start.1
  19.3 4.5 collective-permute-start.2
  24.4 4.8 %collective-permute-start.3 = (bf16[1,1,2,32,256]{4,2,3,1,0:T(2,128)(2,1)}, bf16[1,1,2,32,256]{4,2,3,1,0:T(2,128)(2,1)S(1)}, u32[]{:S(2)}, u32[]{:S(2)}) collective-permute-start(bf16[1,1,2,32,256]{4,2,3,1,0:T(2,128)(2,1)} %copy.86), channel_id=1, source_target_pairs={{0,128},{32,160},{64,192},{96,224},{128,256},{160,288},{192,320},{... | collective-permute-start | bytes 98312 | tf_op jit(solution)/shard_map/ppermute | solution.py:25
  31.4 3.0 reshape.500
  36.7 3.0 reshape.501
  42.1 3.7 collective-permute-start.5
  47.2 5.9 %collective-permute-start.6 = (bf16[1,1,2,32,256]{4,2,3,1,0:T(2,128)(2,1)S(1)}, bf16[1,1,2,32,256]{4,2,3,1,0:T(2,128)(2,1)S(1)}, u32[]{:S(2)}, u32[]{:S(2)}) collective-permute-start(bf16[1,1,2,32,256]{4,2,3,1,0:T(2,128)(2,1)S(1)} %copy.89), channel_id=1, source_target_pairs={{0,224},{32,256},{64,288},{96,320},{128,352},{160,384},{192,416},{... | collective-permute-start | bytes 98312 | tf_op jit(solution)/shard_map/ppermute | solution.py:25
  54.5 3.8 collective-permute-start.7
  59.8 5.4 %collective-permute-start.8 = (bf16[1,1,2,32,256]{4,2,3,1,0:T(2,128)(2,1)S(1)}, bf16[1,1,2,32,256]{4,2,3,1,0:T(2,128)(2,1)S(1)}, u32[]{:S(2)}, u32[]{:S(2)}) collective-permute-start(bf16[1,1,2,32,256]{4,2,3,1,0:T(2,128)(2,1)S(1)} %copy.91), channel_id=1, source_target_pairs={{0,288},{32,320},{64,352},{96,384},{128,416},{160,448},{192,480},{... | collective-permute-start | bytes 98312 | tf_op jit(solution)/shard_map/ppermute | solution.py:25
  65.8 3.9 collective-permute-start.9
  70.3 3.5 collective-permute-start.10
  74.5 4.0 collective-permute-start.11
  79.2 4.7 %collective-permute-start.12 = (bf16[1,1,2,32,256]{4,2,3,1,0:T(2,128)(2,1)S(1)}, bf16[1,1,2,32,256]{4,2,3,1,0:T(2,128)(2,1)S(1)}, u32[]{:S(2)}, u32[]{:S(2)}) collective-permute-start(bf16[1,1,2,32,256]{4,2,3,1,0:T(2,128)(2,1)S(1)} %copy.95), channel_id=1, source_target_pairs={{0,416},{32,448},{64,480},{96,0},{128,32},{160,64},{192,96},{224,1... | collective-permute-start | bytes 98312 | tf_op jit(solution)/shard_map/ppermute | solution.py:25
  84.5 3.2 collective-permute-start.13
  92.8 13.5 %all-to-all-start = ((bf16[16,2,32,256]{3,1,0,2:T(2,128)(2,1)}), bf16[16,2,32,256]{3,1,0,2:T(2,128)(2,1)S(1)}, u32[]{:S(2)}, u32[]{:S(2)}) async-start(bf16[16,2,32,256]{3,1,0,2:T(2,128)(2,1)} %bitcast_dynamic-update-slice_fusion), calls=%async_computation | async-start | bytes 1048576 | tf_op jit(solution)/shard_map/all_to_all | solution.py:65
  106.6 30.4 %scatter_custom_fusion.1 = s32[1025]{0:T(1024)S(1)} fusion(s32[8192]{0:T(1024)S(1)} %bitcast.70, s32[8192]{0:T(1024)S(1)} %reshape.581, s32[]{:T(128)} %constant.339.clone.1), kind=kCustom, calls=%fused_computation.115 | custom fusion | bytes 4104 | tf_op jit(solution)/shard_map/scatter | solution.py:82
  137.5 4.9 %gather_fusion.3 = bf16[1024,256]{1,0:T(8,128)(2,1)} fusion(bf16[1025,256]{1,0:T(8,128)(2,1)S(1)} %concatenate.10, s32[1024]{0:T(1024)S(1)} %fusion.30), kind=kCustom, calls=%fused_computation.clone | custom fusion | bytes 1052672 | tf_op jit(solution)/shard_map/jit(_take)/gather | solution.py:95
  151.4 30.4 %scatter_custom_fusion = s32[1025]{0:T(1024)S(1)} fusion(s32[8192]{0:T(1024)S(1)} %bitcast.69, s32[8192]{0:T(1024)S(1)} %fusion.7, s32[]{:T(128)} %constant.339.clone.1), kind=kCustom, calls=%fused_computation.117 | custom fusion | bytes 4104 | tf_op jit(solution)/shard_map/scatter | solution.py:87
  186.5 30.4 %scatter_custom_fusion.2 = f32[1025]{0:T(1024)S(1)} fusion(s32[8192]{0:T(1024)S(1)} %bitcast.71, f32[8192]{0:T(1024)S(1)} %reshape.589, f32[]{:T(128)} %constant.373.clone.1), kind=kCustom, calls=%fused_computation.106 | custom fusion | bytes 4104 | tf_op jit(solution)/shard_map/scatter | solution.py:92
  216.9 84.3 %all-reduce.4.cloned.1.call-done = bf16[8,128,512]{2,1,0:T(8,128)(2,1)} async-done(((bf16[8,128,512]{2,1,0:T(8,128)(2,1)}), bf16[8,128,512]{2,1,0:T(8,128)(2,1)}) %all-reduce.4.cloned.1.call-update) | async-done | bytes 1048592 | tf_op jit(solution)/shard_map/psum | solution.py:100
  301.3 3.4 fusion.36
  304.7 6.8 %gather_fusion = bf16[1024]{0:T(1024)(128)(2,1)S(1)} fusion(bf16[1025]{0:T(1024)(128)(2,1)S(1)} %pad_maximum_fusion, s32[1024]{0:T(1024)S(1)} %get-tuple-element.44), kind=kCustom, calls=%fused_computation.2 | custom fusion | bytes 8192 | tf_op jit(solution)/shard_map/jit(_take)/gather | solution.py:131
  312.2 6.8 %all-to-all-start.1 = ((bf16[16,2,32]{2,1,0:T(2,128)(2,1)}), bf16[16,2,32]{2,1,0:T(2,128)(2,1)S(1)}, u32[]{:S(2)}, u32[]{:S(2)}) async-start(bf16[16,2,32]{2,1,0:T(2,128)(2,1)} %and_select_fusion.2), calls=%async_computation.1 | async-start | bytes 16384 | tf_op jit(solution)/shard_map/all_to_all | solution.py:134
  321.4 5.0 %gather_fusion.4 = bf16[1024,256]{1,0:T(8,128)(2,1)} fusion(bf16[1025,256]{1,0:T(8,128)(2,1)S(1)} %concatenate.12, s32[1024]{0:T(1024)S(1)} %get-tuple-element.44), kind=kCustom, calls=%fused_computation.1.clone | custom fusion | bytes 1052672 | tf_op jit(solution)/shard_map/jit(_take)/gather | solution.py:128
  328.4 7.2 %all-to-all-start.2 = ((bf16[16,2,32,256]{3,2,1,0:T(8,128)(2,1)}), bf16[16,2,32,256]{3,2,1,0:T(8,128)(2,1)S(1)}, u32[]{:S(2)}, u32[]{:S(2)}) async-start(bf16[16,2,32,256]{3,2,1,0:T(8,128)(2,1)} %bitcast.65), calls=%async_computation.2 | async-start | bytes 1048576 | tf_op jit(solution)/shard_map/all_to_all | solution.py:133
  336.4 3.5 gather_fusion.1
  340.1 11.5 %all-to-all-done.2 = bf16[16,2,32,256]{3,2,1,0:T(8,128)(2,1)S(1)} async-done(((bf16[16,2,32,256]{3,2,1,0:T(8,128)(2,1)}), bf16[16,2,32,256]{3,2,1,0:T(8,128)(2,1)S(1)}, u32[]{:S(2)}, u32[]{:S(2)}) %all-to-all-start.2) | async-done | bytes 524320 | tf_op jit(solution)/shard_map/all_to_all | solution.py:133
  355.7 34.0 %all-gather.2.cloned.1.call-done = bf16[256,8192]{1,0:T(8,128)(2,1)} async-done(((bf16[8,8192]{1,0:T(8,128)(2,1)}), bf16[256,8192]{1,0:T(8,128)(2,1)}) %all-gather.2.cloned.1.call-update) | async-done | bytes 4194320 | tf_op jit(solution)/shard_map/all_gather | solution.py:149
  389.7 5.4 %convolution_convert_fusion = bf16[256,8192]{1,0:T(8,128)(2,1)} fusion(bf16[256,256]{1,0:T(8,128)(2,1)S(1)} %fusion.3, bf16[256,8192]{1,0:T(8,128)(2,1)} %all-gather.2.cloned.1.call-done), kind=kOutput, calls=%fused_computation.8 | convolution fusion | flops 1075838976 | bytes 8519680 | tf_op jit(solution)/shard_map/dot_general | solution.py:147
  395.2 3.8 convolution_convert_fusion.2
  399.6 58.9 %reduce-scatter.2.cloned.1.call-done = bf16[256,512]{1,0:T(8,128)(2,1)} async-done(((bf16[256,8192]{1,0:T(8,128)(2,1)}), bf16[256,512]{1,0:T(8,128)(2,1)}) %reduce-scatter.2.cloned.1.call-update) | async-done | bytes 262160 | tf_op jit(solution)/shard_map/reduce_scatter | solution.py:153
  (123 shorter events, 49.9 us)
Async XLA Ops:
  7.2 136.5 %copy-start = (bf16[8,256,512]{2,1,0:T(8,128)(2,1)S(1)}, bf16[8,256,512]{2,1,0:T(8,128)(2,1)}, u32[]{:S(2)}) copy-start(bf16[8,256,512]{2,1,0:T(8,128)(2,1)} %param.15) | copy-start | bytes 6291460
  7.4 5.8 %copy-start.1 = (bf16[8,8192]{1,0:T(8,128)(2,1)S(1)}, bf16[8,8192]{1,0:T(8,128)(2,1)}, u32[]{:S(2)}) copy-start(bf16[8,8192]{1,0:T(8,128)(2,1)} %param.10) | copy-start | bytes 393220
  13.7 21.1 %copy-start.2 = (s32[4096,2]{0,1:T(2,128)S(1)}, s32[4096,2]{0,1:T(2,128)}, u32[]{:S(2)}) copy-start(s32[4096,2]{0,1:T(2,128)} %param.13) | copy-start | bytes 98308
  14.5 27.6 %collective-permute-start = (bf16[1,1,2,32,256]{4,2,3,1,0:T(2,128)(2,1)}, bf16[1,1,2,32,256]{4,2,3,1,0:T(2,128)(2,1)}, u32[]{:S(2)}, u32[]{:S(2)}) collective-permute-start(bf16[1,1,2,32,256]{4,2,3,1,0:T(2,128)(2,1)} %copy.83), channel_id=1, source_target_pairs={{0,32},{32,64},{64,96},{96,128},{128,160},{160,192},{192,224},{224... | collective-permute-start | bytes 98312 | tf_op jit(solution)/shard_map/ppermute | solution.py:25
  15.1 32.0 %collective-permute-start.1 = (bf16[1,1,2,32,256]{4,2,3,1,0:T(2,128)(2,1)}, bf16[1,1,2,32,256]{4,2,3,1,0:T(2,128)(2,1)}, u32[]{:S(2)}, u32[]{:S(2)}) collective-permute-start(bf16[1,1,2,32,256]{4,2,3,1,0:T(2,128)(2,1)} %copy.84), channel_id=1, source_target_pairs={{0,64},{32,96},{64,128},{96,160},{128,192},{160,224},{192,256},{22... | collective-permute-start | bytes 98312 | tf_op jit(solution)/shard_map/ppermute | solution.py:25
  19.3 35.3 %collective-permute-start.2 = (bf16[1,1,2,32,256]{4,2,3,1,0:T(2,128)(2,1)}, bf16[1,1,2,32,256]{4,2,3,1,0:T(2,128)(2,1)}, u32[]{:S(2)}, u32[]{:S(2)}) collective-permute-start(bf16[1,1,2,32,256]{4,2,3,1,0:T(2,128)(2,1)} %copy.85), channel_id=1, source_target_pairs={{0,96},{32,128},{64,160},{96,192},{128,224},{160,256},{192,288},{2... | collective-permute-start | bytes 98312 | tf_op jit(solution)/shard_map/ppermute | solution.py:25
  24.4 35.4 %collective-permute-start.3 = (bf16[1,1,2,32,256]{4,2,3,1,0:T(2,128)(2,1)}, bf16[1,1,2,32,256]{4,2,3,1,0:T(2,128)(2,1)S(1)}, u32[]{:S(2)}, u32[]{:S(2)}) collective-permute-start(bf16[1,1,2,32,256]{4,2,3,1,0:T(2,128)(2,1)} %copy.86), channel_id=1, source_target_pairs={{0,128},{32,160},{64,192},{96,224},{128,256},{160,288},{192,320},{... | collective-permute-start | bytes 98312 | tf_op jit(solution)/shard_map/ppermute | solution.py:25
  29.2 36.5 %collective-permute-start.4 = (bf16[1,1,2,32,256]{4,2,3,1,0:T(2,128)(2,1)S(1)}, bf16[1,1,2,32,256]{4,2,3,1,0:T(2,128)(2,1)S(1)}, u32[]{:S(2)}, u32[]{:S(2)}) collective-permute-start(bf16[1,1,2,32,256]{4,2,3,1,0:T(2,128)(2,1)S(1)} %copy.87), channel_id=1, source_target_pairs={{0,160},{32,192},{64,224},{96,256},{128,288},{160,320},{192,352},{... | collective-permute-start | bytes 98312 | tf_op jit(solution)/shard_map/ppermute | solution.py:25
  42.1 28.2 %collective-permute-start.5 = (bf16[1,1,2,32,256]{4,2,3,1,0:T(2,128)(2,1)S(1)}, bf16[1,1,2,32,256]{4,2,3,1,0:T(2,128)(2,1)S(1)}, u32[]{:S(2)}, u32[]{:S(2)}) collective-permute-start(bf16[1,1,2,32,256]{4,2,3,1,0:T(2,128)(2,1)S(1)} %copy.88), channel_id=1, source_target_pairs={{0,192},{32,224},{64,256},{96,288},{128,320},{160,352},{192,384},{... | collective-permute-start | bytes 98312 | tf_op jit(solution)/shard_map/ppermute | solution.py:25
  47.2 27.4 %collective-permute-start.6 = (bf16[1,1,2,32,256]{4,2,3,1,0:T(2,128)(2,1)S(1)}, bf16[1,1,2,32,256]{4,2,3,1,0:T(2,128)(2,1)S(1)}, u32[]{:S(2)}, u32[]{:S(2)}) collective-permute-start(bf16[1,1,2,32,256]{4,2,3,1,0:T(2,128)(2,1)S(1)} %copy.89), channel_id=1, source_target_pairs={{0,224},{32,256},{64,288},{96,320},{128,352},{160,384},{192,416},{... | collective-permute-start | bytes 98312 | tf_op jit(solution)/shard_map/ppermute | solution.py:25
  54.5 24.6 %collective-permute-start.7 = (bf16[1,1,2,32,256]{4,2,3,1,0:T(2,128)(2,1)S(1)}, bf16[1,1,2,32,256]{4,2,3,1,0:T(2,128)(2,1)S(1)}, u32[]{:S(2)}, u32[]{:S(2)}) collective-permute-start(bf16[1,1,2,32,256]{4,2,3,1,0:T(2,128)(2,1)S(1)} %copy.90), channel_id=1, source_target_pairs={{0,256},{32,288},{64,320},{96,352},{128,384},{160,416},{192,448},{... | collective-permute-start | bytes 98312 | tf_op jit(solution)/shard_map/ppermute | solution.py:25
  59.8 24.8 %collective-permute-start.8 = (bf16[1,1,2,32,256]{4,2,3,1,0:T(2,128)(2,1)S(1)}, bf16[1,1,2,32,256]{4,2,3,1,0:T(2,128)(2,1)S(1)}, u32[]{:S(2)}, u32[]{:S(2)}) collective-permute-start(bf16[1,1,2,32,256]{4,2,3,1,0:T(2,128)(2,1)S(1)} %copy.91), channel_id=1, source_target_pairs={{0,288},{32,320},{64,352},{96,384},{128,416},{160,448},{192,480},{... | collective-permute-start | bytes 98312 | tf_op jit(solution)/shard_map/ppermute | solution.py:25
  65.8 22.6 %collective-permute-start.9 = (bf16[1,1,2,32,256]{4,2,3,1,0:T(2,128)(2,1)S(1)}, bf16[1,1,2,32,256]{4,2,3,1,0:T(2,128)(2,1)S(1)}, u32[]{:S(2)}, u32[]{:S(2)}) collective-permute-start(bf16[1,1,2,32,256]{4,2,3,1,0:T(2,128)(2,1)S(1)} %copy.92), channel_id=1, source_target_pairs={{0,320},{32,352},{64,384},{96,416},{128,448},{160,480},{192,0},{22... | collective-permute-start | bytes 98312 | tf_op jit(solution)/shard_map/ppermute | solution.py:25
  70.3 19.3 %collective-permute-start.10 = (bf16[1,1,2,32,256]{4,2,3,1,0:T(2,128)(2,1)S(1)}, bf16[1,1,2,32,256]{4,2,3,1,0:T(2,128)(2,1)S(1)}, u32[]{:S(2)}, u32[]{:S(2)}) collective-permute-start(bf16[1,1,2,32,256]{4,2,3,1,0:T(2,128)(2,1)S(1)} %copy.93), channel_id=1, source_target_pairs={{0,352},{32,384},{64,416},{96,448},{128,480},{160,0},{192,32},{224... | collective-permute-start | bytes 98312 | tf_op jit(solution)/shard_map/ppermute | solution.py:25
  74.5 15.7 %collective-permute-start.11 = (bf16[1,1,2,32,256]{4,2,3,1,0:T(2,128)(2,1)S(1)}, bf16[1,1,2,32,256]{4,2,3,1,0:T(2,128)(2,1)S(1)}, u32[]{:S(2)}, u32[]{:S(2)}) collective-permute-start(bf16[1,1,2,32,256]{4,2,3,1,0:T(2,128)(2,1)S(1)} %copy.94), channel_id=1, source_target_pairs={{0,384},{32,416},{64,448},{96,480},{128,0},{160,32},{192,64},{224,... | collective-permute-start | bytes 98312 | tf_op jit(solution)/shard_map/ppermute | solution.py:25
  79.2 11.7 %collective-permute-start.12 = (bf16[1,1,2,32,256]{4,2,3,1,0:T(2,128)(2,1)S(1)}, bf16[1,1,2,32,256]{4,2,3,1,0:T(2,128)(2,1)S(1)}, u32[]{:S(2)}, u32[]{:S(2)}) collective-permute-start(bf16[1,1,2,32,256]{4,2,3,1,0:T(2,128)(2,1)S(1)} %copy.95), channel_id=1, source_target_pairs={{0,416},{32,448},{64,480},{96,0},{128,32},{160,64},{192,96},{224,1... | collective-permute-start | bytes 98312 | tf_op jit(solution)/shard_map/ppermute | solution.py:25
  84.5 7.0 %collective-permute-start.13 = (bf16[1,1,2,32,256]{4,2,3,1,0:T(2,128)(2,1)S(1)}, bf16[1,1,2,32,256]{4,2,3,1,0:T(2,128)(2,1)S(1)}, u32[]{:S(2)}, u32[]{:S(2)}) collective-permute-start(bf16[1,1,2,32,256]{4,2,3,1,0:T(2,128)(2,1)S(1)} %copy.96), channel_id=1, source_target_pairs={{0,448},{32,480},{64,0},{96,32},{128,64},{160,96},{192,128},{224,1... | collective-permute-start | bytes 98312 | tf_op jit(solution)/shard_map/ppermute | solution.py:25
  88.4 3.8 collective-permute-start.14
  92.8 44.3 %all-to-all-start = ((bf16[16,2,32,256]{3,1,0,2:T(2,128)(2,1)}), bf16[16,2,32,256]{3,1,0,2:T(2,128)(2,1)S(1)}, u32[]{:S(2)}, u32[]{:S(2)}) async-start(bf16[16,2,32,256]{3,1,0,2:T(2,128)(2,1)} %bitcast_dynamic-update-slice_fusion), calls=%async_computation | async-start | bytes 1048576 | tf_op jit(solution)/shard_map/all_to_all | solution.py:65
  106.3 195.0 %all-reduce.4.cloned.1.call-start = ((), (), s32[]{:S(2)}) async-start(), calls=%async_computation.4 | async-start | bytes 2097152 | tf_op jit(solution)/shard_map/psum | solution.py:100
  145.1 244.6 %all-gather.2.cloned.1.call-start = ((), (), s32[]{:S(2)}) async-start(), calls=%async_computation.5 | async-start | bytes 4325376 | tf_op jit(solution)/shard_map/all_gather | solution.py:149
  145.9 36.1 %copy-start.3 = (bf16[4096,2]{0,1:T(2,128)(2,1)S(1)}, bf16[4096,2]{0,1:T(2,128)(2,1)}, u32[]{:S(2)}) copy-start(bf16[4096,2]{0,1:T(2,128)(2,1)} %param.14) | copy-start | bytes 49156
  182.0 119.3 %copy-start.4 = (f32[8,512]{1,0:T(8,128)S(1)}, f32[8,512]{1,0:T(8,128)}, u32[]{:S(2)}) copy-start(f32[8,512]{1,0:T(8,128)} %param.16) | copy-start | bytes 49156
  182.0 119.3 %copy-start.5 = (f32[8,512]{1,0:T(8,128)S(1)}, f32[8,512]{1,0:T(8,128)}, u32[]{:S(2)}) copy-start(f32[8,512]{1,0:T(8,128)} %param.17) | copy-start | bytes 49156
  312.2 16.3 %all-to-all-start.1 = ((bf16[16,2,32]{2,1,0:T(2,128)(2,1)}), bf16[16,2,32]{2,1,0:T(2,128)(2,1)S(1)}, u32[]{:S(2)}, u32[]{:S(2)}) async-start(bf16[16,2,32]{2,1,0:T(2,128)(2,1)} %and_select_fusion.2), calls=%async_computation.1 | async-start | bytes 16384 | tf_op jit(solution)/shard_map/all_to_all | solution.py:134
  328.4 23.2 %all-to-all-start.2 = ((bf16[16,2,32,256]{3,2,1,0:T(8,128)(2,1)}), bf16[16,2,32,256]{3,2,1,0:T(8,128)(2,1)S(1)}, u32[]{:S(2)}, u32[]{:S(2)}) async-start(bf16[16,2,32,256]{3,2,1,0:T(8,128)(2,1)} %bitcast.65), calls=%async_computation.2 | async-start | bytes 1048576 | tf_op jit(solution)/shard_map/all_to_all | solution.py:133
  335.7 122.9 %reduce-scatter.2.cloned.1.call-start = ((), (), s32[]{:S(2)}) async-start(), calls=%async_computation.6 | async-start | bytes 4456448 | tf_op jit(solution)/shard_map/reduce_scatter | solution.py:153
Sparse Core Ops, SparseCore 0:
  145.3 155.9 all-reduce.3
  304.4 85.2 all-gather.1
  395.3 63.2 reduce-scatter.1
